TPU v7x, 32 devices: a whole 2x2x4 slice. The times are simulated.
32 devices in a mesh: query: 2 (over x), gallery: 16 (over z, y, core).
Axes of the slice: x: 2, y: 2, z: 4, core: 2. Of those that a mesh axis runs over, the one named last changes fastest.
Arguments:
- query_hidden: bfloat16 [768, 32, 768], P(('query', 'gallery')), may hold values from -6 to 6
- query_mask: int32 [768, 32], P(('query', 'gallery')), may hold values 0 or 1
- passage_hidden: bfloat16 [16, 360, 768], P('gallery', 'query'), may hold values from -6 to 6
- passage_ids: int32 [16, 360], P('gallery', 'query'), may hold values from 999 to 30521, as said below
- passage_lengths: int32 [32], P('gallery'), may hold values from 30 to 180, as said below
- projection: bfloat16 [768, 128], replicated, may hold values from -0.21875 to 0.21875
Outputs:
- scores: float32 [768, 32], P(('query', 'gallery'))
Inputs may be any that keep to these rules, and one draw needn't show every extreme that they name: `passage_ids`: ids from 999 to 1066 are punctuation; the rest are words. `passage_lengths`: some passage has exactly 180 tokens.
All inputs are finite; a program needn't handle non-finite values. No bound on the sum of `query_mask` on one device may be relied on, other than what follows from the above.
Results may differ from a plain program's by a relative error of at most 0.00036.
Values may be sent and summed in bfloat16 or wider, within the bound.
A program may use at most 64 MiB of HBM per device.

v0:
```python
import math
import jax
import jax.numpy as jnp
from jax import lax
from jax.sharding import PartitionSpec as P

DIM = 128
PLEN = 180
QLEN = 32
PUNCT_LO = 999
PUNCT_HI = 1067
PASS_GRP = 2
EPS = 1e-06
NEG = -1000000000.0


def unit_rows(hidden, projection):
    flat_rows = hidden.reshape(-1, hidden.shape[-1])
    projected = jnp.dot(flat_rows, projection, preferred_element_type=jnp.float32)
    inverse_norm = lax.rsqrt(jnp.sum(projected * projected, axis=-1, keepdims=True) + EPS)
    return (projected * inverse_norm).astype(jnp.bfloat16)


def local(query_hidden, query_mask, passage_hidden, passage_ids, passage_lengths, projection):
    row_count = passage_hidden.shape[1]
    query_count = query_hidden.shape[0]
    groups = lax.axis_size("gallery")
    query_block = lax.axis_index("query")
    position = query_block * row_count + jnp.arange(row_count, dtype=jnp.int32)
    passage_slot = position // PLEN
    token_pos = position % PLEN
    onehot = passage_slot[:, None] == jnp.arange(PASS_GRP, dtype=jnp.int32)[None, :]
    length_rows = jnp.sum(jnp.where(onehot, passage_lengths[None, :], 0), axis=1)
    token_ids = passage_ids[0]
    punctuation = (token_ids >= PUNCT_LO) & (token_ids < PUNCT_HI)
    kept = (token_pos < length_rows) & ((token_pos == 0) | jnp.logical_not(punctuation))
    kept_flag = kept.astype(jnp.bfloat16)[None, :]
    passage_unit = unit_rows(passage_hidden, projection).reshape(1, row_count, DIM)
    query_unit = unit_rows(query_hidden, projection)
    weights = query_mask.astype(jnp.float32).reshape(-1)
    thin_units, thin_flags = (
        lax.all_gather(passage_unit, "gallery", axis=0, tiled=True),
        lax.all_gather(kept_flag, "gallery", axis=0, tiled=True),
    )
    initial = jnp.full((query_unit.shape[0], groups * PASS_GRP), NEG, jnp.float32)
    piece_units = lax.all_gather(thin_units, "query", axis=1, tiled=True)
    piece_flags = lax.all_gather(thin_flags, "query", axis=1, tiled=True)
    piece_rows = piece_units.shape[1]
    row_slot = jnp.arange(piece_rows, dtype=jnp.int32) // PLEN
    block_width = math.gcd(groups, 4)
    unit_blocks = piece_units.reshape(groups // block_width, block_width * piece_rows, DIM)
    flag_blocks = piece_flags.reshape(groups // block_width, 1, block_width * piece_rows)

    def one_block(block_pair):
        unit_block, flag_block = block_pair
        similar = jnp.einsum(
            "td,rd->tr", query_unit, unit_block, preferred_element_type=jnp.float32
        )
        similar = jnp.where(flag_block > 0, similar, NEG).reshape(-1, block_width, piece_rows)
        per_member = [
            jnp.max(jnp.where(row_slot == member, similar, NEG), axis=2)
            for member in range(PASS_GRP)
        ]
        return jnp.stack(per_member, axis=2)

    fresh_max = lax.map(one_block, (unit_blocks, flag_blocks))
    fresh_max = jnp.transpose(fresh_max, (1, 0, 2, 3)).reshape(initial.shape)
    running = jnp.maximum(initial, fresh_max)
    scores = jnp.sum(
        (running * weights[:, None]).reshape(query_count, QLEN, groups * PASS_GRP), axis=1
    )
    return scores


def solution(mesh):
    placed = (
        P(("query", "gallery"), None, None),
        P(("query", "gallery"), None),
        P("gallery", "query", None),
        P("gallery", "query"),
        P("gallery"),
        P(),
    )
    return jax.shard_map(
        local, mesh=mesh, in_specs=placed, out_specs=P(("query", "gallery"), None), check_vma=False
    )
```

profile of v0, /device:TPU:0, one launch (start us, length us, event | category | flops | bytes accessed | tf_op | source)
XLA Modules:
  0.0 77.6 jit_solution(7608371529911874838)
XLA Ops:
  6.5 1.4 %multiply_reduce_fusion.2 = (f32[180]{0:T(256)S(1)}, f32[180,128]{1,0:T(8,128)S(1)}) fusion(bf16[768,128]{1,0:T(8,128)(2,1)} %param.13, bf16[1,180,768]{2,1,0:T(8,128)(2,1)} %param.10), kind=kOutput, calls=%fused_computation.26 | convolution fusion | flops 35435340 | bytes 565968 | tf_op jit(solution)/shard_map/dot_general | solution.py:19
  8.0 0.1 fusion.11
  8.1 25.5 %all-gather.3 = bf16[16,180,128]{2,1,0:T(8,128)(2,1)S(1)} all-gather(bf16[1,180,128]{2,1,0:T(8,128)(2,1)S(1)} %fusion.11), channel_id=2, replica_groups=mesh['query'=2,'gallery'=16] {'gallery'}, dimensions={0}, use_global_device_ids=true | all-gather | bytes 783360 | tf_op jit(solution)/shard_map/all_gather | solution.py:42
  33.6 1.0 %copy.25 = bf16[16,180,128]{2,0,1:T(8,128)(2,1)} copy(bf16[16,180,128]{2,1,0:T(8,128)(2,1)S(1)} %all-gather.3) | data formatting | bytes 1474560 | tf_op jit(solution)/shard_map/all_gather | solution.py:42
  34.7 0.6 multiply_reduce_fusion.1
  35.3 0.2 copy.28
  35.6 17.5 %all-gather.1 = bf16[16,1,180]{2,1,0:T(2,128)(2,1)S(1)} all-gather(bf16[1,1,180]{2,1,0:T(2,128)(2,1)S(1)} %fusion.13), channel_id=1, replica_groups=mesh['query'=2,'gallery'=16] {'gallery'}, dimensions={0}, use_global_device_ids=true | all-gather | bytes 6120 | tf_op jit(solution)/shard_map/all_gather | solution.py:43
  53.1 4.5 %all-gather.2 = bf16[2,180,16]{1,2,0:T(8,128)(2,1)S(1)} all-gather(bf16[1,180,16]{1,2,0:T(8,128)(2,1)S(1)} %bitcast.56), channel_id=1, replica_groups=mesh['query'=2,'gallery'=16] {'query'}, dimensions={0}, use_global_device_ids=true | all-gather | bytes 17280 | tf_op jit(solution)/shard_map/all_gather | solution.py:47
  57.6 0.1 reshape.108
  57.7 0.1 reshape.113
  57.8 0.5 all-gather.6.cloned.1.call-done
  58.3 1.8 %copy.26 = bf16[16,360,128]{2,1,0:T(8,128)(2,1)S(1)} copy(bf16[16,360,128]{2,0,1:T(8,128)(2,1)} %all-gather.6.cloned.1.call-done) | data formatting | bytes 2949120 | tf_op jit(solution)/shard_map/all_gather | solution.py:46
  60.1 9.6 %while.12 = (s32[]{:T(128)}, f32[4,768,4,2]{1,3,2,0:T(2,128)S(1)}, bf16[4,1,1440]{2,1,0:T(2,128)(2,1)S(1)}, bf16[4,1440,128]{2,1,0:T(8,128)(2,1)S(1)}, bf16[768,128]{1,0:T(8,128)(2,1)S(1)}, /*index=5*/s32[]{:T(128)}) while((s32[]{:T(128)}, f32[4,768,4,2]{1,3,2,0:T(2,128)S(1)}, bf16[4,1,1440]{2,1,0:T(2,128)(2,1)S(1)}, ...), condition=%wide.region_6.7_spmd.clone.clone, body=%wide.region_3.6_spmd.clone.clone.sunk | while | flops 288650176 | bytes 9543377 | solution.py:66
  60.2 1.1 %convolution_select_fusion.2 = f32[1440,768]{1,0:T(8,128)S(1)} fusion(bf16[768,128]{1,0:T(8,128)(2,1)S(1)} %get-tuple-element.172, pred[1440]{0:T(1024)(128)(4,1)S(1)} %compare_reduce_fusion.2, bf16[4,1440,128]{2,1,0:T(8,128)(2,1)S(1)} %get-tuple-element.171, s32[]{:T(128)} %get-tuple-element.162), kind=kOutput, calls=%fused_computation.3.clone.1 | convolution fusion | flops 284221440 | bytes 4990980 | tf_op jit(solution)/shard_map/while/body/eval_jaxpr/td,rd->tr/dot_general | solution.py:56
  61.3 1.1 %select_reduce_fusion.3 = (f32[768,4]{0,1:T(4,128)S(1)}, f32[768,4]{0,1:T(4,128)S(1)}) fusion(f32[768,4,360]{0,2,1:T(8,128)S(1)} %bitcast.53, pred[360]{0:T(512)(128)(4,1)S(1)} %get-tuple-element.152, pred[360]{0:T(512)(128)(4,1)S(1)} %get-tuple-element.153), kind=kLoop, calls=%fused_computation.2.clone.1 | loop fusion | flops 4417536 | bytes 4448976 | tf_op jit(solution)/shard_map/while/body/eval_jaxpr/reduce_max | solution.py:61
  62.5 1.1 %convolution_select_fusion.2 = f32[1440,768]{1,0:T(8,128)S(1)} fusion(bf16[768,128]{1,0:T(8,128)(2,1)S(1)} %get-tuple-element.172, pred[1440]{0:T(1024)(128)(4,1)S(1)} %compare_reduce_fusion.2, bf16[4,1440,128]{2,1,0:T(8,128)(2,1)S(1)} %get-tuple-element.171, s32[]{:T(128)} %get-tuple-element.162), kind=kOutput, calls=%fused_computation.3.clone.1 | convolution fusion | flops 284221440 | bytes 4990980 | tf_op jit(solution)/shard_map/while/body/eval_jaxpr/td,rd->tr/dot_general | solution.py:56
  63.7 1.1 %select_reduce_fusion.3 = (f32[768,4]{0,1:T(4,128)S(1)}, f32[768,4]{0,1:T(4,128)S(1)}) fusion(f32[768,4,360]{0,2,1:T(8,128)S(1)} %bitcast.53, pred[360]{0:T(512)(128)(4,1)S(1)} %get-tuple-element.152, pred[360]{0:T(512)(128)(4,1)S(1)} %get-tuple-element.153), kind=kLoop, calls=%fused_computation.2.clone.1 | loop fusion | flops 4417536 | bytes 4448976 | tf_op jit(solution)/shard_map/while/body/eval_jaxpr/reduce_max | solution.py:61
  64.9 1.1 %convolution_select_fusion.2 = f32[1440,768]{1,0:T(8,128)S(1)} fusion(bf16[768,128]{1,0:T(8,128)(2,1)S(1)} %get-tuple-element.172, pred[1440]{0:T(1024)(128)(4,1)S(1)} %compare_reduce_fusion.2, bf16[4,1440,128]{2,1,0:T(8,128)(2,1)S(1)} %get-tuple-element.171, s32[]{:T(128)} %get-tuple-element.162), kind=kOutput, calls=%fused_computation.3.clone.1 | convolution fusion | flops 284221440 | bytes 4990980 | tf_op jit(solution)/shard_map/while/body/eval_jaxpr/td,rd->tr/dot_general | solution.py:56
  66.1 1.1 %select_reduce_fusion.3 = (f32[768,4]{0,1:T(4,128)S(1)}, f32[768,4]{0,1:T(4,128)S(1)}) fusion(f32[768,4,360]{0,2,1:T(8,128)S(1)} %bitcast.53, pred[360]{0:T(512)(128)(4,1)S(1)} %get-tuple-element.152, pred[360]{0:T(512)(128)(4,1)S(1)} %get-tuple-element.153), kind=kLoop, calls=%fused_computation.2.clone.1 | loop fusion | flops 4417536 | bytes 4448976 | tf_op jit(solution)/shard_map/while/body/eval_jaxpr/reduce_max | solution.py:61
  67.3 1.1 %convolution_select_fusion.2 = f32[1440,768]{1,0:T(8,128)S(1)} fusion(bf16[768,128]{1,0:T(8,128)(2,1)S(1)} %get-tuple-element.172, pred[1440]{0:T(1024)(128)(4,1)S(1)} %compare_reduce_fusion.2, bf16[4,1440,128]{2,1,0:T(8,128)(2,1)S(1)} %get-tuple-element.171, s32[]{:T(128)} %get-tuple-element.162), kind=kOutput, calls=%fused_computation.3.clone.1 | convolution fusion | flops 284221440 | bytes 4990980 | tf_op jit(solution)/shard_map/while/body/eval_jaxpr/td,rd->tr/dot_general | solution.py:56
  68.5 1.1 %select_reduce_fusion.3 = (f32[768,4]{0,1:T(4,128)S(1)}, f32[768,4]{0,1:T(4,128)S(1)}) fusion(f32[768,4,360]{0,2,1:T(8,128)S(1)} %bitcast.53, pred[360]{0:T(512)(128)(4,1)S(1)} %get-tuple-element.152, pred[360]{0:T(512)(128)(4,1)S(1)} %get-tuple-element.153), kind=kLoop, calls=%fused_computation.2.clone.1 | loop fusion | flops 4417536 | bytes 4448976 | tf_op jit(solution)/shard_map/while/body/eval_jaxpr/reduce_max | solution.py:61
  69.7 0.2 max_broadcast_in_dim.12
  69.9 0.2 multiply_reduce_fusion
  70.1 0.7 copy.29
  (43 shorter events, 0.7 us)
Async XLA Ops:
  6.5 28.1 %copy-start = (bf16[24,32,768]{2,1,0:T(8,128)(2,1)S(1)}, bf16[24,32,768]{2,1,0:T(8,128)(2,1)}, u32[]{:S(2)}) copy-start(bf16[24,32,768]{2,1,0:T(8,128)(2,1)} %param.8) | copy-start | bytes 3538948
  6.5 51.8 %all-gather.6.cloned.1.call-start = ((), (), s32[]{:S(2)}) async-start(), calls=%async_computation | async-start | bytes 2211840 | tf_op jit(solution)/shard_map/all_gather | solution.py:46
  8.1 26.6 %copy-start.1 = (bf16[768,128]{1,0:T(8,128)(2,1)S(1)}, bf16[768,128]{1,0:T(8,128)(2,1)}, u32[]{:S(2)}) copy-start(bf16[768,128]{1,0:T(8,128)(2,1)} %param.13) | copy-start | bytes 589828
  34.6 0.9 %copy-start.4 = (s32[2]{0:T(128)S(1)}, s32[2]{0:T(128)}, u32[]{:S(2)}) copy-start(s32[2]{0:T(128)} %param.12) | copy-start | bytes 28
  34.6 1.0 %copy-start.3 = (s32[1,180]{1,0:T(1,128)S(1)}, s32[1,180]{1,0:T(1,128)}, u32[]{:S(2)}) copy-start(s32[1,180]{1,0:T(1,128)} %param.11) | copy-start | bytes 2164
  34.7 23.1 %copy-start.2 = (s32[24,32]{1,0:T(8,128)S(1)}, s32[24,32]{1,0:T(8,128)}, u32[]{:S(2)}) copy-start(s32[24,32]{1,0:T(8,128)} %param.9) | copy-start | bytes 9220
Sparse Core Ops, SparseCore 0:
  34.7 23.5 all-gather.5
where the time goes:
time: 77.8 us; the launch traced here: 77.6 us
  blocking collectives  47.5 us (61%)
  between operations  13.6 us (17%)
  matrix products  6.51 us (8%)
  other arithmetic  5.26 us (7%)
  local copies, waits for them, and re-layouts  4.07 us (5%)
    all_gather x1, blocking collectives, local(): lax.all_gather(passage_unit, 'gallery', axis=0, tiled=True)  25.5 us
    all_gather x1, blocking collectives, local(): lax.all_gather(kept_flag, 'gallery', axis=0, tiled=True)  17.5 us
    dot_general x4, matrix products, one_block(): jnp.einsum('td,rd->tr', query_unit, unit_block, preferred_element_type=jn...  4.52 us
    all_gather x1, blocking collectives, local(): piece_flags = lax.all_gather(thin_flags, 'query', axis=1, tiled=True)  4.49 us
    reduce_max x4, other arithmetic, one_block(): jnp.max(jnp.where(row_slot == member, similar, NEG), axis=2)  4.39 us
    dot_general x2, matrix products, unit_rows(): jnp.dot(flat_rows, projection, preferred_element_type=jnp.float32)  2 us
    all_gather x1, local copies, waits for them, and re-layouts, local(): piece_units = lax.all_gather(thin_units, 'query', axis=1, tiled=True)  1.75 us
  transfers between devices with their start and end apart: 1, of which 1 were waited for; matrix products, arithmetic and copies ran while one was open for 1% of the time, Pallas kernels for 0%

commit v1 on v0

--- a/solution.py
+++ b/solution.py
@@ -12,6 +12,24 @@
 PASS_GRP = 2
 EPS = 1e-06
 NEG = -1000000000.0
+
+
+def collect(shard, axis, dim):
+    ways, here, step = (lax.axis_size(axis), lax.axis_index(axis), shard.shape[dim])
+    shape = [n * ways if d == dim else n for d, n in enumerate(shard.shape)]
+    full = lax.dynamic_update_slice_in_dim(
+        jnp.zeros(shape, shard.dtype), shard, here * step, axis=dim
+    )
+    going_up = going_down = shard
+    for far in range(1, ways // 2 + 1):
+        going_up = lax.ppermute(going_up, axis, [(d, (d + 1) % ways) for d in range(ways)])
+        full = lax.dynamic_update_slice_in_dim(full, going_up, (here - far) % ways * step, axis=dim)
+        if 2 * far < ways:
+            going_down = lax.ppermute(going_down, axis, [(d, (d - 1) % ways) for d in range(ways)])
+            full = lax.dynamic_update_slice_in_dim(
+                full, going_down, (here + far) % ways * step, axis=dim
+            )
+    return full
 
 
 def unit_rows(hidden, projection):
@@ -40,7 +58,7 @@
     weights = query_mask.astype(jnp.float32).reshape(-1)
     thin_units, thin_flags = (
         lax.all_gather(passage_unit, "gallery", axis=0, tiled=True),
-        lax.all_gather(kept_flag, "gallery", axis=0, tiled=True),
+        collect(kept_flag, "gallery", 0),
     )
     initial = jnp.full((query_unit.shape[0], groups * PASS_GRP), NEG, jnp.float32)
     piece_units = lax.all_gather(thin_units, "query", axis=1, tiled=True)

time: 77.8 us -> 104 us (1.34)
  starting transfers between devices: 0.01 us -> 31 us
  blocking collectives: 47.5 us -> 29.7 us
  waiting for transfers between devices: 0.54 us -> 13.3 us
    ppermute x0 -> x15, starting transfers between devices: none -> 31 us  [the longest x7 30.5 us: collect(): lax.ppermute(going_down, axis, [(d, (d - 1) % ways) for d in range(ways)])]
    all_gather x1 -> x0, blocking collectives: 17.5 us -> none  [local(): lax.all_gather(kept_flag, 'gallery', axis=0, tiled=True)]
    ppermute x0 -> x15, waiting for transfers between devices: none -> 13.2 us  [the longest x8 11.9 us: collect(): lax.ppermute(going_up, axis, [(d, (d + 1) % ways) for d in range(ways)])]
  transfers between devices with their start and end apart: 1 -> 16, of which waited for: 1 -> 14; matrix products, arithmetic and copies ran while one was open for 1% -> 2% of each run, Pallas kernels for 0% -> 0%
where the time goes in v1:
time: 104 us
  starting transfers between devices  31 us (30%)
  blocking collectives  29.7 us (29%)
  between operations  13.6 us (13%)
  waiting for transfers between devices  13.3 us (13%)
  matrix products  6.51 us (6%)
  other arithmetic  5.26 us (5%)
  local copies, waits for them, and re-layouts  4.57 us (4%)
    ppermute x7, starting transfers between devices, collect(): lax.ppermute(going_down, axis, [(d, (d - 1) % ways) for d in range(ways)])  30.5 us
    all_gather x1, blocking collectives, local(): lax.all_gather(passage_unit, 'gallery', axis=0, tiled=True)  25.4 us
    ppermute x8, waiting for transfers between devices, collect(): lax.ppermute(going_up, axis, [(d, (d + 1) % ways) for d in range(ways)])  11.9 us
    dot_general x4, matrix products, one_block(): jnp.einsum('td,rd->tr', query_unit, unit_block, preferred_element_type=jn...  4.51 us
    reduce_max x4, other arithmetic, one_block(): jnp.max(jnp.where(row_slot == member, similar, NEG), axis=2)  4.39 us
    all_gather x1, blocking collectives, local(): piece_flags = lax.all_gather(thin_flags, 'query', axis=1, tiled=True)  4.36 us
  transfers between devices with their start and end apart: 16, of which 14 were waited for; matrix products, arithmetic and copies ran while one was open for 2% of the time, Pallas kernels for 0%

profile of v1, /device:TPU:0, one launch (start us, length us, event | category | flops | bytes accessed | tf_op | source)
XLA Modules:
  0.0 104.1 jit_solution(13159822991051044894)
XLA Ops:
  6.5 1.4 %multiply_reduce_fusion.2 = (f32[180]{0:T(256)S(1)}, f32[180,128]{1,0:T(8,128)S(1)}) fusion(bf16[768,128]{1,0:T(8,128)(2,1)} %param.13, bf16[1,180,768]{2,1,0:T(8,128)(2,1)} %param.10), kind=kOutput, calls=%fused_computation.26 | convolution fusion | flops 35435340 | bytes 565968 | tf_op jit(solution)/shard_map/dot_general | solution.py:37
  8.1 25.4 %all-gather.2 = bf16[16,180,128]{2,1,0:T(8,128)(2,1)S(1)} all-gather(bf16[1,180,128]{2,1,0:T(8,128)(2,1)S(1)} %fusion.11), channel_id=2, replica_groups=mesh['query'=2,'gallery'=16] {'gallery'}, dimensions={0}, use_global_device_ids=true | all-gather | bytes 783360 | tf_op jit(solution)/shard_map/all_gather | solution.py:60
  35.0 4.1 %collective-permute-start.1 = (bf16[1,180]{1,0:T(2,128)(2,1)S(1)}, bf16[1,180]{1,0:T(2,128)(2,1)S(1)}, u32[]{:S(2)}, u32[]{:S(2)}) collective-permute-start(bf16[1,180]{1,0:T(2,128)(2,1)S(1)} %and_convert_fusion), channel_id=1, source_target_pairs={{0,15},{1,0},{2,1},{3,2},{4,3},{5,4},{6,5},{7,6},{8,7},{9,8},{10,9... | collective-permute-start | bytes 1088 | tf_op jit(solution)/shard_map/ppermute | solution.py:28
  40.6 4.5 %collective-permute-start.3 = (bf16[1,180]{1,0:T(2,128)(2,1)S(1)}, bf16[1,180]{1,0:T(2,128)(2,1)S(1)}, u32[]{:S(2)}, u32[]{:S(2)}) collective-permute-start(bf16[1,180]{1,0:T(2,128)(2,1)S(1)} %collective-permute-done.1), channel_id=1, source_target_pairs={{0,15},{1,0},{2,1},{3,2},{4,3},{5,4},{6,5},{7,6},{8,7},{9,8},{10,9... | collective-permute-start | bytes 1088 | tf_op jit(solution)/shard_map/ppermute | solution.py:28
  45.1 1.0 collective-permute-done.2
  46.4 4.4 %collective-permute-start.5 = (bf16[1,180]{1,0:T(2,128)(2,1)S(1)}, bf16[1,180]{1,0:T(2,128)(2,1)S(1)}, u32[]{:S(2)}, u32[]{:S(2)}) collective-permute-start(bf16[1,180]{1,0:T(2,128)(2,1)S(1)} %collective-permute-done.3), channel_id=1, source_target_pairs={{0,15},{1,0},{2,1},{3,2},{4,3},{5,4},{6,5},{7,6},{8,7},{9,8},{10,9... | collective-permute-start | bytes 1088 | tf_op jit(solution)/shard_map/ppermute | solution.py:28
  50.8 1.0 collective-permute-done.4
  52.1 4.4 %collective-permute-start.7 = (bf16[1,180]{1,0:T(2,128)(2,1)S(1)}, bf16[1,180]{1,0:T(2,128)(2,1)S(1)}, u32[]{:S(2)}, u32[]{:S(2)}) collective-permute-start(bf16[1,180]{1,0:T(2,128)(2,1)S(1)} %collective-permute-done.5), channel_id=1, source_target_pairs={{0,15},{1,0},{2,1},{3,2},{4,3},{5,4},{6,5},{7,6},{8,7},{9,8},{10,9... | collective-permute-start | bytes 1088 | tf_op jit(solution)/shard_map/ppermute | solution.py:28
  56.5 1.0 collective-permute-done.6
  57.8 4.4 %collective-permute-start.9 = (bf16[1,180]{1,0:T(2,128)(2,1)S(1)}, bf16[1,180]{1,0:T(2,128)(2,1)S(1)}, u32[]{:S(2)}, u32[]{:S(2)}) collective-permute-start(bf16[1,180]{1,0:T(2,128)(2,1)S(1)} %collective-permute-done.7), channel_id=1, source_target_pairs={{0,15},{1,0},{2,1},{3,2},{4,3},{5,4},{6,5},{7,6},{8,7},{9,8},{10,9... | collective-permute-start | bytes 1088 | tf_op jit(solution)/shard_map/ppermute | solution.py:28
  63.5 4.4 %collective-permute-start.11 = (bf16[1,180]{1,0:T(2,128)(2,1)S(1)}, bf16[1,180]{1,0:T(2,128)(2,1)S(1)}, u32[]{:S(2)}, u32[]{:S(2)}) collective-permute-start(bf16[1,180]{1,0:T(2,128)(2,1)S(1)} %collective-permute-done.9), channel_id=1, source_target_pairs={{0,15},{1,0},{2,1},{3,2},{4,3},{5,4},{6,5},{7,6},{8,7},{9,8},{10,9... | collective-permute-start | bytes 1088 | tf_op jit(solution)/shard_map/ppermute | solution.py:28
  69.1 4.4 %collective-permute-start.13 = (bf16[1,180]{1,0:T(2,128)(2,1)S(1)}, bf16[1,180]{1,0:T(2,128)(2,1)S(1)}, u32[]{:S(2)}, u32[]{:S(2)}) collective-permute-start(bf16[1,180]{1,0:T(2,128)(2,1)S(1)} %collective-permute-done.11), channel_id=1, source_target_pairs={{0,15},{1,0},{2,1},{3,2},{4,3},{5,4},{6,5},{7,6},{8,7},{9,8},{10,9... | collective-permute-start | bytes 1088 | tf_op jit(solution)/shard_map/ppermute | solution.py:28
  74.9 5.4 %collective-permute-done.14 = bf16[1,180]{1,0:T(2,128)(2,1)S(1)} collective-permute-done((bf16[1,180]{1,0:T(2,128)(2,1)S(1)}, bf16[1,180]{1,0:T(2,128)(2,1)S(1)}, u32[]{:S(2)}, u32[]{:S(2)}) %collective-permute-start.14) | collective-permute-done | bytes 392 | tf_op jit(solution)/shard_map/ppermute | solution.py:25
  80.2 4.4 %all-gather.1 = bf16[2,180,16]{1,2,0:T(8,128)(2,1)S(1)} all-gather(bf16[1,180,16]{1,2,0:T(8,128)(2,1)S(1)} %bitcast.50), channel_id=1, replica_groups=mesh['query'=2,'gallery'=16] {'query'}, dimensions={0}, use_global_device_ids=true | all-gather | bytes 17280 | tf_op jit(solution)/shard_map/all_gather | solution.py:65
  84.8 1.8 %copy.26 = bf16[16,360,128]{2,1,0:T(8,128)(2,1)S(1)} copy(bf16[16,360,128]{2,0,1:T(8,128)(2,1)} %all-gather.5.cloned.1.call-done) | data formatting | bytes 2949120 | tf_op jit(solution)/shard_map/all_gather | solution.py:64
  86.6 9.6 %while.12 = (s32[]{:T(128)}, f32[4,768,4,2]{1,3,2,0:T(2,128)S(1)}, bf16[4,1,1440]{2,1,0:T(2,128)(2,1)S(1)}, bf16[4,1440,128]{2,1,0:T(8,128)(2,1)S(1)}, bf16[768,128]{1,0:T(8,128)(2,1)S(1)}, /*index=5*/s32[]{:T(128)}) while((s32[]{:T(128)}, f32[4,768,4,2]{1,3,2,0:T(2,128)S(1)}, bf16[4,1,1440]{2,1,0:T(2,128)(2,1)S(1)}, ...), condition=%wide.region_6.7_spmd.clone.clone, body=%wide.region_3.6_spmd.clone.clone.sunk | while | flops 288650176 | bytes 9543377 | solution.py:84
  86.6 1.1 %convolution_select_fusion.2 = f32[1440,768]{1,0:T(8,128)S(1)} fusion(bf16[768,128]{1,0:T(8,128)(2,1)S(1)} %get-tuple-element.172, pred[1440]{0:T(1024)(128)(4,1)S(1)} %compare_reduce_fusion.2, bf16[4,1440,128]{2,1,0:T(8,128)(2,1)S(1)} %get-tuple-element.171, s32[]{:T(128)} %get-tuple-element.162), kind=kOutput, calls=%fused_computation.3.clone.1 | convolution fusion | flops 284221440 | bytes 4990980 | tf_op jit(solution)/shard_map/while/body/eval_jaxpr/td,rd->tr/dot_general | solution.py:74
  87.8 1.1 %select_reduce_fusion.3 = (f32[768,4]{0,1:T(4,128)S(1)}, f32[768,4]{0,1:T(4,128)S(1)}) fusion(f32[768,4,360]{0,2,1:T(8,128)S(1)} %bitcast.47, pred[360]{0:T(512)(128)(4,1)S(1)} %get-tuple-element.152, pred[360]{0:T(512)(128)(4,1)S(1)} %get-tuple-element.153), kind=kLoop, calls=%fused_computation.2.clone.1 | loop fusion | flops 4417536 | bytes 4448976 | tf_op jit(solution)/shard_map/while/body/eval_jaxpr/reduce_max | solution.py:79
  89.0 1.1 %convolution_select_fusion.2 = f32[1440,768]{1,0:T(8,128)S(1)} fusion(bf16[768,128]{1,0:T(8,128)(2,1)S(1)} %get-tuple-element.172, pred[1440]{0:T(1024)(128)(4,1)S(1)} %compare_reduce_fusion.2, bf16[4,1440,128]{2,1,0:T(8,128)(2,1)S(1)} %get-tuple-element.171, s32[]{:T(128)} %get-tuple-element.162), kind=kOutput, calls=%fused_computation.3.clone.1 | convolution fusion | flops 284221440 | bytes 4990980 | tf_op jit(solution)/shard_map/while/body/eval_jaxpr/td,rd->tr/dot_general | solution.py:74
  90.2 1.1 %select_reduce_fusion.3 = (f32[768,4]{0,1:T(4,128)S(1)}, f32[768,4]{0,1:T(4,128)S(1)}) fusion(f32[768,4,360]{0,2,1:T(8,128)S(1)} %bitcast.47, pred[360]{0:T(512)(128)(4,1)S(1)} %get-tuple-element.152, pred[360]{0:T(512)(128)(4,1)S(1)} %get-tuple-element.153), kind=kLoop, calls=%fused_computation.2.clone.1 | loop fusion | flops 4417536 | bytes 4448976 | tf_op jit(solution)/shard_map/while/body/eval_jaxpr/reduce_max | solution.py:79
  91.4 1.1 %convolution_select_fusion.2 = f32[1440,768]{1,0:T(8,128)S(1)} fusion(bf16[768,128]{1,0:T(8,128)(2,1)S(1)} %get-tuple-element.172, pred[1440]{0:T(1024)(128)(4,1)S(1)} %compare_reduce_fusion.2, bf16[4,1440,128]{2,1,0:T(8,128)(2,1)S(1)} %get-tuple-element.171, s32[]{:T(128)} %get-tuple-element.162), kind=kOutput, calls=%fused_computation.3.clone.1 | convolution fusion | flops 284221440 | bytes 4990980 | tf_op jit(solution)/shard_map/while/body/eval_jaxpr/td,rd->tr/dot_general | solution.py:74
  92.6 1.1 %select_reduce_fusion.3 = (f32[768,4]{0,1:T(4,128)S(1)}, f32[768,4]{0,1:T(4,128)S(1)}) fusion(f32[768,4,360]{0,2,1:T(8,128)S(1)} %bitcast.47, pred[360]{0:T(512)(128)(4,1)S(1)} %get-tuple-element.152, pred[360]{0:T(512)(128)(4,1)S(1)} %get-tuple-element.153), kind=kLoop, calls=%fused_computation.2.clone.1 | loop fusion | flops 4417536 | bytes 4448976 | tf_op jit(solution)/shard_map/while/body/eval_jaxpr/reduce_max | solution.py:79
  93.8 1.1 %convolution_select_fusion.2 = f32[1440,768]{1,0:T(8,128)S(1)} fusion(bf16[768,128]{1,0:T(8,128)(2,1)S(1)} %get-tuple-element.172, pred[1440]{0:T(1024)(128)(4,1)S(1)} %compare_reduce_fusion.2, bf16[4,1440,128]{2,1,0:T(8,128)(2,1)S(1)} %get-tuple-element.171, s32[]{:T(128)} %get-tuple-element.162), kind=kOutput, calls=%fused_computation.3.clone.1 | convolution fusion | flops 284221440 | bytes 4990980 | tf_op jit(solution)/shard_map/while/body/eval_jaxpr/td,rd->tr/dot_general | solution.py:74
  95.0 1.1 %select_reduce_fusion.3 = (f32[768,4]{0,1:T(4,128)S(1)}, f32[768,4]{0,1:T(4,128)S(1)}) fusion(f32[768,4,360]{0,2,1:T(8,128)S(1)} %bitcast.47, pred[360]{0:T(512)(128)(4,1)S(1)} %get-tuple-element.152, pred[360]{0:T(512)(128)(4,1)S(1)} %get-tuple-element.153), kind=kLoop, calls=%fused_computation.2.clone.1 | loop fusion | flops 4417536 | bytes 4448976 | tf_op jit(solution)/shard_map/while/body/eval_jaxpr/reduce_max | solution.py:79
  (88 shorter events, 9.6 us)
Async XLA Ops:
  6.5 32.6 %copy-start = (bf16[24,32,768]{2,1,0:T(8,128)(2,1)S(1)}, bf16[24,32,768]{2,1,0:T(8,128)(2,1)}, u32[]{:S(2)}) copy-start(bf16[24,32,768]{2,1,0:T(8,128)(2,1)} %param.8) | copy-start | bytes 3538948
  6.5 78.3 %all-gather.5.cloned.1.call-start = ((), (), s32[]{:S(2)}) async-start(), calls=%async_computation | async-start | bytes 2211840 | tf_op jit(solution)/shard_map/all_gather | solution.py:64
  8.1 26.4 %copy-start.4 = (s32[2]{0:T(128)S(1)}, s32[2]{0:T(128)}, u32[]{:S(2)}) copy-start(s32[2]{0:T(128)} %param.12) | copy-start | bytes 28
  8.1 26.5 %copy-start.3 = (s32[1,180]{1,0:T(1,128)S(1)}, s32[1,180]{1,0:T(1,128)}, u32[]{:S(2)}) copy-start(s32[1,180]{1,0:T(1,128)} %param.11) | copy-start | bytes 2164
  33.5 5.6 %copy-start.1 = (bf16[768,128]{1,0:T(8,128)(2,1)S(1)}, bf16[768,128]{1,0:T(8,128)(2,1)}, u32[]{:S(2)}) copy-start(bf16[768,128]{1,0:T(8,128)(2,1)} %param.13) | copy-start | bytes 589828
  34.6 5.7 %collective-permute-start = (bf16[1,180]{1,0:T(2,128)(2,1)S(1)}, bf16[1,180]{1,0:T(2,128)(2,1)S(1)}, u32[]{:S(2)}, u32[]{:S(2)}) collective-permute-start(bf16[1,180]{1,0:T(2,128)(2,1)S(1)} %and_convert_fusion), channel_id=1, source_target_pairs={{0,1},{1,2},{2,3},{3,4},{4,5},{5,6},{6,7},{7,8},{8,9},{9,10},{10,1... | collective-permute-start | bytes 1088 | tf_op jit(solution)/shard_map/ppermute | solution.py:25
  35.0 5.5 %collective-permute-start.1 = (bf16[1,180]{1,0:T(2,128)(2,1)S(1)}, bf16[1,180]{1,0:T(2,128)(2,1)S(1)}, u32[]{:S(2)}, u32[]{:S(2)}) collective-permute-start(bf16[1,180]{1,0:T(2,128)(2,1)S(1)} %and_convert_fusion), channel_id=1, source_target_pairs={{0,15},{1,0},{2,1},{3,2},{4,3},{5,4},{6,5},{7,6},{8,7},{9,8},{10,9... | collective-permute-start | bytes 1088 | tf_op jit(solution)/shard_map/ppermute | solution.py:28
  39.1 1.4 %copy-start.2 = (s32[24,32]{1,0:T(8,128)S(1)}, s32[24,32]{1,0:T(8,128)}, u32[]{:S(2)}) copy-start(s32[24,32]{1,0:T(8,128)} %param.9) | copy-start | bytes 9220
  40.4 5.7 %collective-permute-start.2 = (bf16[1,180]{1,0:T(2,128)(2,1)S(1)}, bf16[1,180]{1,0:T(2,128)(2,1)S(1)}, u32[]{:S(2)}, u32[]{:S(2)}) collective-permute-start(bf16[1,180]{1,0:T(2,128)(2,1)S(1)} %collective-permute-done), channel_id=1, source_target_pairs={{0,1},{1,2},{2,3},{3,4},{4,5},{5,6},{6,7},{7,8},{8,9},{9,10},{10,1... | collective-permute-start | bytes 1088 | tf_op jit(solution)/shard_map/ppermute | solution.py:25
  40.6 5.8 %collective-permute-start.3 = (bf16[1,180]{1,0:T(2,128)(2,1)S(1)}, bf16[1,180]{1,0:T(2,128)(2,1)S(1)}, u32[]{:S(2)}, u32[]{:S(2)}) collective-permute-start(bf16[1,180]{1,0:T(2,128)(2,1)S(1)} %collective-permute-done.1), channel_id=1, source_target_pairs={{0,15},{1,0},{2,1},{3,2},{4,3},{5,4},{6,5},{7,6},{8,7},{9,8},{10,9... | collective-permute-start | bytes 1088 | tf_op jit(solution)/shard_map/ppermute | solution.py:28
  46.1 5.7 %collective-permute-start.4 = (bf16[1,180]{1,0:T(2,128)(2,1)S(1)}, bf16[1,180]{1,0:T(2,128)(2,1)S(1)}, u32[]{:S(2)}, u32[]{:S(2)}) collective-permute-start(bf16[1,180]{1,0:T(2,128)(2,1)S(1)} %collective-permute-done.2), channel_id=1, source_target_pairs={{0,1},{1,2},{2,3},{3,4},{4,5},{5,6},{6,7},{7,8},{8,9},{9,10},{10,1... | collective-permute-start | bytes 1088 | tf_op jit(solution)/shard_map/ppermute | solution.py:25
  46.4 5.7 %collective-permute-start.5 = (bf16[1,180]{1,0:T(2,128)(2,1)S(1)}, bf16[1,180]{1,0:T(2,128)(2,1)S(1)}, u32[]{:S(2)}, u32[]{:S(2)}) collective-permute-start(bf16[1,180]{1,0:T(2,128)(2,1)S(1)} %collective-permute-done.3), channel_id=1, source_target_pairs={{0,15},{1,0},{2,1},{3,2},{4,3},{5,4},{6,5},{7,6},{8,7},{9,8},{10,9... | collective-permute-start | bytes 1088 | tf_op jit(solution)/shard_map/ppermute | solution.py:28
  51.8 5.7 %collective-permute-start.6 = (bf16[1,180]{1,0:T(2,128)(2,1)S(1)}, bf16[1,180]{1,0:T(2,128)(2,1)S(1)}, u32[]{:S(2)}, u32[]{:S(2)}) collective-permute-start(bf16[1,180]{1,0:T(2,128)(2,1)S(1)} %collective-permute-done.4), channel_id=1, source_target_pairs={{0,1},{1,2},{2,3},{3,4},{4,5},{5,6},{6,7},{7,8},{8,9},{9,10},{10,1... | collective-permute-start | bytes 1088 | tf_op jit(solution)/shard_map/ppermute | solution.py:25
  52.1 5.7 %collective-permute-start.7 = (bf16[1,180]{1,0:T(2,128)(2,1)S(1)}, bf16[1,180]{1,0:T(2,128)(2,1)S(1)}, u32[]{:S(2)}, u32[]{:S(2)}) collective-permute-start(bf16[1,180]{1,0:T(2,128)(2,1)S(1)} %collective-permute-done.5), channel_id=1, source_target_pairs={{0,15},{1,0},{2,1},{3,2},{4,3},{5,4},{6,5},{7,6},{8,7},{9,8},{10,9... | collective-permute-start | bytes 1088 | tf_op jit(solution)/shard_map/ppermute | solution.py:28
  57.4 5.7 %collective-permute-start.8 = (bf16[1,180]{1,0:T(2,128)(2,1)S(1)}, bf16[1,180]{1,0:T(2,128)(2,1)S(1)}, u32[]{:S(2)}, u32[]{:S(2)}) collective-permute-start(bf16[1,180]{1,0:T(2,128)(2,1)S(1)} %collective-permute-done.6), channel_id=1, source_target_pairs={{0,1},{1,2},{2,3},{3,4},{4,5},{5,6},{6,7},{7,8},{8,9},{9,10},{10,1... | collective-permute-start | bytes 1088 | tf_op jit(solution)/shard_map/ppermute | solution.py:25
  57.8 5.7 %collective-permute-start.9 = (bf16[1,180]{1,0:T(2,128)(2,1)S(1)}, bf16[1,180]{1,0:T(2,128)(2,1)S(1)}, u32[]{:S(2)}, u32[]{:S(2)}) collective-permute-start(bf16[1,180]{1,0:T(2,128)(2,1)S(1)} %collective-permute-done.7), channel_id=1, source_target_pairs={{0,15},{1,0},{2,1},{3,2},{4,3},{5,4},{6,5},{7,6},{8,7},{9,8},{10,9... | collective-permute-start | bytes 1088 | tf_op jit(solution)/shard_map/ppermute | solution.py:28
  63.1 5.7 %collective-permute-start.10 = (bf16[1,180]{1,0:T(2,128)(2,1)S(1)}, bf16[1,180]{1,0:T(2,128)(2,1)S(1)}, u32[]{:S(2)}, u32[]{:S(2)}) collective-permute-start(bf16[1,180]{1,0:T(2,128)(2,1)S(1)} %collective-permute-done.8), channel_id=1, source_target_pairs={{0,1},{1,2},{2,3},{3,4},{4,5},{5,6},{6,7},{7,8},{8,9},{9,10},{10,1... | collective-permute-start | bytes 1088 | tf_op jit(solution)/shard_map/ppermute | solution.py:25
  63.5 5.7 %collective-permute-start.11 = (bf16[1,180]{1,0:T(2,128)(2,1)S(1)}, bf16[1,180]{1,0:T(2,128)(2,1)S(1)}, u32[]{:S(2)}, u32[]{:S(2)}) collective-permute-start(bf16[1,180]{1,0:T(2,128)(2,1)S(1)} %collective-permute-done.9), channel_id=1, source_target_pairs={{0,15},{1,0},{2,1},{3,2},{4,3},{5,4},{6,5},{7,6},{8,7},{9,8},{10,9... | collective-permute-start | bytes 1088 | tf_op jit(solution)/shard_map/ppermute | solution.py:28
  68.8 5.7 %collective-permute-start.12 = (bf16[1,180]{1,0:T(2,128)(2,1)S(1)}, bf16[1,180]{1,0:T(2,128)(2,1)S(1)}, u32[]{:S(2)}, u32[]{:S(2)}) collective-permute-start(bf16[1,180]{1,0:T(2,128)(2,1)S(1)} %collective-permute-done.10), channel_id=1, source_target_pairs={{0,1},{1,2},{2,3},{3,4},{4,5},{5,6},{6,7},{7,8},{8,9},{9,10},{10,1... | collective-permute-start | bytes 1088 | tf_op jit(solution)/shard_map/ppermute | solution.py:25
  69.1 5.7 %collective-permute-start.13 = (bf16[1,180]{1,0:T(2,128)(2,1)S(1)}, bf16[1,180]{1,0:T(2,128)(2,1)S(1)}, u32[]{:S(2)}, u32[]{:S(2)}) collective-permute-start(bf16[1,180]{1,0:T(2,128)(2,1)S(1)} %collective-permute-done.11), channel_id=1, source_target_pairs={{0,15},{1,0},{2,1},{3,2},{4,3},{5,4},{6,5},{7,6},{8,7},{9,8},{10,9... | collective-permute-start | bytes 1088 | tf_op jit(solution)/shard_map/ppermute | solution.py:28
  74.5 5.7 %collective-permute-start.14 = (bf16[1,180]{1,0:T(2,128)(2,1)S(1)}, bf16[1,180]{1,0:T(2,128)(2,1)S(1)}, u32[]{:S(2)}, u32[]{:S(2)}) collective-permute-start(bf16[1,180]{1,0:T(2,128)(2,1)S(1)} %collective-permute-done.12), channel_id=1, source_target_pairs={{0,1},{1,2},{2,3},{3,4},{4,5},{5,6},{6,7},{7,8},{8,9},{9,10},{10,1... | collective-permute-start | bytes 1088 | tf_op jit(solution)/shard_map/ppermute | solution.py:25
Sparse Core Ops, SparseCore 0:
  34.6 23.3 all-gather.4
